TPU v7x, 32 devices: a whole 2x2x4 slice. The times are simulated.
32 devices in a mesh: grp: 4 (over y, core), feat: 8 (over z, x).
Axes of the slice: x: 2, y: 2, z: 4, core: 2. Of those that a mesh axis runs over, the one named last changes fastest.
Arguments:
- features: bfloat16 [128, 16384], P('feat', 'grp'), may hold values from -6 to 6
- w_self: bfloat16 [128, 256], replicated, may hold values from -0.5 to 0.5
- w_neigh: bfloat16 [128, 256], replicated, may hold values from -0.5 to 0.5
- bias: float32 [256], replicated, may hold values from -3 to 3
- tile_vals: bfloat16 [4, 8, 8, 128, 128], P('grp'), may hold values from -0.5 to 0.5
- tile_src: int32 [4, 8, 8], P('grp'), may hold values from 0 to 39, as said below
- tile_dst: int32 [4, 8, 8], P('grp'), may hold values from 0 to 3
- tile_count: int32 [4, 8], P('grp'), may hold values from 1 to 8, as said below
- hub_blocks: int32 [4, 2], P('grp'), may hold values from 0 to 31, as said below
- cotangent: bfloat16 [16384, 256], P(('grp', 'feat')), may hold values from -6 to 6
Outputs:
- output: bfloat16 [16384, 256], P(('grp', 'feat'))
- feat_grad: float32 [128, 16384], P('feat', 'grp')
- wself_grad: float32 [128, 256], P('feat')
- wneigh_grad: float32 [128, 256], P('feat')
- bias_grad: float32 [256], replicated
Inputs may be any that keep to these rules, and one draw needn't show every extreme that they name: `tile_src`: a slot number of the tile's own group's blocks below 32, or 32 plus a hub number. `tile_count`: some owner uses all 8 slots in every draw. `hub_blocks`: the 2 block numbers of a group are distinct.
All inputs are finite; a program needn't handle non-finite values.
Results may differ from a plain program's by a relative error of at most 0.0055.
Values may be sent and summed in bfloat16 or wider, within the bound.
A program may use at most 128 MiB of HBM per device.

v0:
```python
import jax
import jax.numpy as jnp
from jax import lax
from jax.sharding import PartitionSpec as P


def silu_parts(preact):
    sig = jax.nn.sigmoid(preact)
    return (preact * sig, sig * (1.0 + preact * (1.0 - sig)))


def contract_first(left, right):
    return lax.dot_general(
        left, right, (((0,), (0,)), ((), ())), preferred_element_type=jnp.float32
    )


def contract_last(left, right):
    return lax.dot_general(
        left, right, (((1,), (1,)), ((), ())), preferred_element_type=jnp.float32
    )


def local(
    features,
    w_self,
    w_neigh,
    bias,
    tile_vals,
    tile_src,
    tile_dst,
    tile_count,
    hub_blocks,
    cotangent,
):
    columns, group_nodes = features.shape
    owners = lax.axis_size("feat")
    position = lax.axis_index("feat")
    slot_count = tile_src.shape[2]
    tile_size = tile_vals.shape[-1]
    group_blocks = group_nodes // tile_size
    own_blocks = group_blocks // owners
    row_count = own_blocks * tile_size
    hub_ids = hub_blocks[0]
    highest = lax.Precision.HIGHEST
    own_hubs = jnp.take(
        features.reshape(columns, group_blocks, tile_size), hub_ids, axis=1
    ).reshape(columns, -1)
    all_hubs = lax.all_gather(own_hubs, "grp", axis=1, tiled=True)
    slot_total = group_blocks + all_hubs.shape[1] // tile_size
    upstream = cotangent.astype(jnp.float32)
    combined = jnp.concatenate([features, all_hubs], axis=1)
    full = lax.all_gather(combined, "feat", axis=0, tiled=True)
    feat_total = full.shape[0]
    values = lax.dynamic_index_in_dim(tile_vals[0], position, 0, keepdims=False)
    src_ids = lax.dynamic_index_in_dim(tile_src[0], position, 0, keepdims=False)
    dst_ids = lax.dynamic_index_in_dim(tile_dst[0], position, 0, keepdims=False)
    live_count = lax.dynamic_index_in_dim(tile_count[0], position, 0, keepdims=False)
    live_slots = (jnp.arange(slot_count, dtype=jnp.int32) < live_count).astype(jnp.float32)
    picked = jnp.take(full.reshape(feat_total, slot_total, tile_size), src_ids, axis=1)
    contrib = (
        jnp.einsum("tds,fts->ftd", values, picked, preferred_element_type=jnp.float32)
        * live_slots[None, :, None]
    )
    dst_hot = (dst_ids[:, None] == jnp.arange(own_blocks, dtype=jnp.int32)[None, :]).astype(
        jnp.float32
    )
    agg_own = (
        jnp.einsum("ftd,tb->fbd", contrib, dst_hot, precision=highest)
        .reshape(feat_total, row_count)
        .astype(jnp.bfloat16)
    )
    feat_own = lax.dynamic_slice_in_dim(full, position * row_count, row_count, 1)
    preact = contract_first(feat_own, w_self) + contract_first(agg_own, w_neigh) + bias
    activated, slope = silu_parts(preact)
    output = activated.astype(jnp.bfloat16)
    grad_pre = (upstream * slope).astype(jnp.bfloat16)
    wself_full = jnp.dot(feat_own, grad_pre, preferred_element_type=jnp.float32)
    wneigh_full = jnp.dot(agg_own, grad_pre, preferred_element_type=jnp.float32)
    bias_grad = jnp.sum(grad_pre.astype(jnp.float32), axis=0)
    wself_full, wneigh_full, bias_grad = lax.psum(
        (wself_full, wneigh_full, bias_grad), ("grp", "feat")
    )
    wself_grad = lax.dynamic_slice_in_dim(wself_full, position * columns, columns, 0)
    wneigh_grad = lax.dynamic_slice_in_dim(wneigh_full, position * columns, columns, 0)
    self_grad = contract_last(w_self, grad_pre)
    agg_grad = contract_last(w_neigh, grad_pre).astype(jnp.bfloat16)
    chosen = jnp.take(agg_grad.reshape(feat_total, own_blocks, tile_size), dst_ids, axis=1)
    src_grad = (
        jnp.einsum("tds,ftd->fts", values, chosen, preferred_element_type=jnp.float32)
        * live_slots[None, :, None]
    )
    src_hot = (src_ids[:, None] == jnp.arange(slot_total, dtype=jnp.int32)[None, :]).astype(
        jnp.float32
    )
    slot_grad = jnp.einsum("fts,tk->fks", src_grad, src_hot, precision=highest).reshape(
        feat_total, slot_total * tile_size
    )
    own_part = lax.dynamic_slice_in_dim(slot_grad, position * row_count, row_count, 1) + self_grad
    slot_grad = lax.dynamic_update_slice_in_dim(slot_grad, own_part, position * row_count, 1)
    mine = lax.psum_scatter(slot_grad, "feat", scatter_dimension=0, tiled=True)
    local_grad = mine[:, :group_nodes]
    hub_part = mine[:, group_nodes:]
    hub_back = (
        lax.psum_scatter(hub_part.astype(jnp.bfloat16), "grp", scatter_dimension=1, tiled=True)
        .astype(jnp.float32)
        .reshape(columns, -1, tile_size)
    )
    local_blocks = local_grad.reshape(columns, group_blocks, tile_size).at[:, hub_ids].add(hub_back)
    feat_grad = local_blocks.reshape(columns, group_nodes)
    return (output, feat_grad, wself_grad, wneigh_grad, bias_grad)


def solution(mesh):
    return jax.shard_map(
        local,
        mesh=mesh,
        in_specs=(
            P("feat", "grp"),
            P(),
            P(),
            P(),
            P("grp", None, None, None, None),
            P("grp", None, None),
            P("grp", None, None),
            P("grp", None),
            P("grp", None),
            P(("grp", "feat"), None),
        ),
        out_specs=(
            P(("grp", "feat"), None),
            P("feat", "grp"),
            P("feat", None),
            P("feat", None),
            P(),
        ),
        check_vma=False,
    )
```

profile of v0, /device:TPU:0, one launch (start us, length us, event | category | flops | bytes accessed | tf_op | source)
XLA Modules:
  0.0 304.6 jit_solution(11308443132222153842)
XLA Ops:
  7.2 0.0 copy-start
  7.2 0.0 all-gather.2.cloned.1.call-start
  7.2 0.8 fusion.38
  8.0 0.7 compare_and_fusion.2
  8.7 0.1 broadcast_bitcast_fusion
  8.8 0.9 copy_bitcast_fusion.3
  9.7 0.6 gather_fusion
  10.3 6.2 %all_gather.6 = bf16[16,1024]{1,0:T(8,128)(2,1)S(1)} all-gather(bf16[16,256]{1,0:T(8,128)(2,1)S(1)} %bitcast_select_fusion), channel_id=1, replica_groups=mesh['grp'=4,'feat'=8] {'grp'}, dimensions={1}, use_global_device_ids=true | all-gather | bytes 40960 | tf_op jit(solution)/shard_map/all_gather | solution.py:49
  16.5 1.6 pad_maximum_fusion
  18.1 0.0 all-gather.2.cloned.1.call-update
  18.1 0.0 all-reduce.3.cloned.1.call-start
  18.2 1.2 constant_dynamic-slice_fusion.3
  19.4 0.6 compare_convert_fusion
  20.1 0.7 fusion.39
  20.8 0.7 fusion.40
  21.5 0.7 compare_and_fusion
  22.2 39.8 %all-gather.2.cloned.1.call-done = bf16[128,5120]{1,0:T(8,128)(2,1)} async-done(((bf16[16,5120]{1,0:T(8,128)(2,1)}), bf16[128,5120]{1,0:T(8,128)(2,1)}) %all-gather.2.cloned.1.call-update) | async-done | bytes 1310736 | tf_op jit(solution)/shard_map/all_gather | solution.py:53
  62.0 1.8 copy.37
  63.8 0.0 copy-start.2
  63.8 1.4 copy.38
  65.2 0.0 copy-start.3
  65.2 0.0 copy-start.4
  65.2 0.0 copy-start.5
  65.2 2.0 gather_fusion.1
  67.2 0.0 copy-done
  67.2 0.4 fusion.1
  67.5 0.7 convolution_convert_fusion.1
  68.2 0.0 copy-done.2
  68.2 1.2 fusion.26
  69.4 0.0 copy-done.3
  69.4 0.0 copy-done.4
  69.4 0.0 copy-done.5
  69.4 1.2 convert_reduce_fusion
  70.6 0.9 fusion.17
  71.4 0.2 convolution_convert_fusion
  71.7 0.1 copy.40
  71.8 0.6 gather_fusion.2
  72.4 0.3 fusion
  72.7 1.3 fusion.4
  74.0 0.5 copy.73
  74.5 0.0 copy-start.1
  74.5 1.5 copy-done.1
  76.0 0.1 copy.47
  76.1 1.8 fusion.24
  77.9 0.0 all-reduce.3.cloned.1.call-update
  77.9 0.0 reduce-scatter.3.cloned.1.call-start
  78.0 0.2 fusion.3
  78.2 0.1 copy.43
  78.3 0.8 constant_dynamic-update-slice_fusion
  79.1 0.0 reduce-scatter.3.cloned.1.call-update
  79.1 0.0 reduce-scatter.5.cloned.1.call-start
  79.2 39.1 %psum.23 = f32[256]{0:T(256)} all-reduce(f32[256]{0:T(256)S(1)} %get-tuple-element.7), channel_id=1, replica_groups=mesh['grp'=4,'feat'=8] {'grp','feat'}, use_global_device_ids=true, to_apply=%region_6.7 | all-reduce | flops 256 | bytes 2048 | tf_op jit(solution)/shard_map/psum | solution.py:81
  118.2 83.7 %all-reduce.3.cloned.1.call-done = (f32[128,256]{1,0:T(8,128)}, f32[128,256]{1,0:T(8,128)}) async-done(((f32[128,256]{1,0:T(8,128)}, f32[128,256]{1,0:T(8,128)}), (f32[128,256]{1,0:T(8,128)}, f32[128,256]{1,0:T(8,128)})) %all-reduce.3.cloned.1.call-update) | async-done | bytes 262160 | tf_op jit(solution)/shard_map/psum | solution.py:81
  201.9 1.3 constant_dynamic-slice_fusion.1
  203.2 1.3 constant_dynamic-slice_fusion
  204.6 70.2 %reduce-scatter.3.cloned.1.call-done = f32[16,5120]{1,0:T(8,128)} async-done(((f32[128,5120]{1,0:T(8,128)}), f32[16,5120]{1,0:T(8,128)}) %reduce-scatter.3.cloned.1.call-update) | async-done | bytes 327696 | tf_op jit(solution)/shard_map/reduce_scatter | solution.py:101
  274.8 1.5 slice.19
  276.3 0.0 reduce-scatter.5.cloned.1.call-update
  276.3 1.0 copy_bitcast_fusion.2
  277.3 18.7 %reduce-scatter.5.cloned.1.call-done = bf16[16,256]{1,0:T(8,128)(2,1)} async-done(((bf16[16,1024]{1,0:T(8,128)(2,1)}), bf16[16,256]{1,0:T(8,128)(2,1)}) %reduce-scatter.5.cloned.1.call-update) | async-done | bytes 8208 | tf_op jit(solution)/shard_map/reduce_scatter | solution.py:105
  296.0 0.7 reshape.194
  296.7 0.6 scatter_fusion
  297.3 0.7 copy_bitcast_fusion.1
  (6 shorter events, 0.0 us)
Async XLA Ops:
  7.2 60.0 %copy-start = (bf16[1,8,8,128,128]{4,3,2,1,0:T(8,128)(2,1)S(1)}, bf16[1,8,8,128,128]{4,3,2,1,0:T(8,128)(2,1)}, u32[]{:S(2)}) copy-start(bf16[1,8,8,128,128]{4,3,2,1,0:T(8,128)(2,1)} %param.14) | copy-start | bytes 6291460
  7.2 54.8 %all-gather.2.cloned.1.call-start = ((), (), s32[]{:S(2)}) async-start(), calls=%async_computation.2 | async-start | bytes 1474560 | tf_op jit(solution)/shard_map/all_gather | solution.py:53
  18.1 183.8 %all-reduce.3.cloned.1.call-start = ((), (), s32[]{:S(2)}) async-start(), calls=%async_computation.5 | async-start | bytes 524288 | tf_op jit(solution)/shard_map/psum | solution.py:81
  63.8 4.5 %copy-start.2 = (bf16[128,256]{1,0:T(8,128)(2,1)S(1)}, bf16[128,256]{1,0:T(8,128)(2,1)}, u32[]{:S(2)}) copy-start(bf16[128,256]{1,0:T(8,128)(2,1)} %param.11) | copy-start | bytes 196612
  65.2 4.2 %copy-start.3 = (bf16[128,256]{1,0:T(8,128)(2,1)S(1)}, bf16[128,256]{1,0:T(8,128)(2,1)}, u32[]{:S(2)}) copy-start(bf16[128,256]{1,0:T(8,128)(2,1)} %param.12) | copy-start | bytes 196612
  65.2 4.2 %copy-start.4 = (bf16[512,256]{1,0:T(8,128)(2,1)S(1)}, bf16[512,256]{1,0:T(8,128)(2,1)}, u32[]{:S(2)}) copy-start(bf16[512,256]{1,0:T(8,128)(2,1)} %param.19) | copy-start | bytes 786436
  65.2 4.2 %copy-start.5 = (f32[256]{0:T(256)S(1)}, f32[256]{0:T(256)}, u32[]{:S(2)}) copy-start(f32[256]{0:T(256)} %param.13) | copy-start | bytes 3076
  74.5 1.5 copy-start.1
  77.9 196.9 %reduce-scatter.3.cloned.1.call-start = ((), (), s32[]{:S(2)}) async-start(), calls=%async_computation.3 | async-start | bytes 2949120 | tf_op jit(solution)/shard_map/reduce_scatter | solution.py:101
  79.1 216.9 %reduce-scatter.5.cloned.1.call-start = ((), (), s32[]{:S(2)}) async-start(), calls=%async_computation.4 | async-start | bytes 40960 | tf_op jit(solution)/shard_map/reduce_scatter | solution.py:105
Sparse Core Ops, SparseCore 0:
  18.2 43.7 all-gather.1
  78.0 123.8 all-reduce.2
  205.4 69.3 reduce-scatter.2
  277.6 18.3 reduce-scatter.4
where the time goes:
time: 305 us
  waiting for transfers between devices  213 us (70%)
  blocking collectives  45.3 us (15%)
  local copies, waits for them, and re-layouts  18.2 us (6%)
  between operations  14 us (5%)
  matrix products  7.97 us (3%)
  other arithmetic  6.42 us (2%)
    psum x1, waiting for transfers between devices, local(): lax.psum((wself_full, wneigh_full, bias_grad), ('grp', 'feat'))  83.7 us
    reduce_scatter x1, waiting for transfers between devices, local(): mine = lax.psum_scatter(slot_grad, 'feat', scatter_dimension=0, tiled=True)  70.2 us
    all_gather x1, waiting for transfers between devices, local(): full = lax.all_gather(combined, 'feat', axis=0, tiled=True)  39.8 us
    psum x1, blocking collectives, local(): lax.psum((wself_full, wneigh_full, bias_grad), ('grp', 'feat'))  39.1 us
    reduce_scatter x1, waiting for transfers between devices, local(): lax.psum_scatter(hub_part.astype(jnp.bfloat16), 'grp', scatter_dimension=...  18.7 us
    all_gather x1, blocking collectives, local(): all_hubs = lax.all_gather(own_hubs, 'grp', axis=1, tiled=True)  6.23 us
  transfers between devices with their start and end apart: 4, of which 4 were waited for; matrix products, arithmetic and copies ran while one was open for 3% of the time, Pallas kernels for 0%

commit v1 on v0

--- a/solution.py
+++ b/solution.py
@@ -50,7 +50,16 @@
     slot_total = group_blocks + all_hubs.shape[1] // tile_size
     upstream = cotangent.astype(jnp.float32)
     combined = jnp.concatenate([features, all_hubs], axis=1)
-    full = lax.all_gather(combined, "feat", axis=0, tiled=True)
+    ways = lax.axis_size("feat")
+    up = [(d, (d + 1) % ways) for d in range(ways)]
+    down = [(d, (d - 1) % ways) for d in range(ways)]
+    earlier, later = ([combined], [combined])
+    for _ in range(ways // 2):
+        earlier.append(lax.ppermute(earlier[-1], "feat", up))
+    for _ in range((ways - 1) // 2):
+        later.append(lax.ppermute(later[-1], "feat", down))
+    line = jnp.concatenate([*earlier[::-1], *later[1:]], axis=0)
+    full = jnp.roll(line, (lax.axis_index("feat") - ways // 2) * combined.shape[0], axis=0)
     feat_total = full.shape[0]
     values = lax.dynamic_index_in_dim(tile_vals[0], position, 0, keepdims=False)
     src_ids = lax.dynamic_index_in_dim(tile_src[0], position, 0, keepdims=False)

time: 305 us -> 273 us (0.90)
  waiting for transfers between devices: 213 us -> 119 us
  local copies, waits for them, and re-layouts: 18.2 us -> 58.3 us
  starting transfers between devices: 0.16 us -> 16.4 us
  blocking collectives: 45.3 us -> 49.3 us
    reduce_scatter x1, waiting for transfers between devices: 70.2 us -> 0.01 us  [local(): mine = lax.psum_scatter(slot_grad, 'feat', scatter_dimension=0, tiled=True)]
    all_gather x1 -> x0, waiting for transfers between devices: 39.8 us -> none  [local(): full = lax.all_gather(combined, 'feat', axis=0, tiled=True)]
    concatenate x0 -> x3, local copies, waits for them, and re-layouts: none -> 21.7 us  [the longest x1 20.2 us: local(): jnp.roll(line, (lax.axis_index('feat') - ways // 2) * combined.shape[0],...]
    ppermute x0 -> x7, local copies, waits for them, and re-layouts: none -> 16.8 us  [the longest x4 9.61 us: local(): earlier.append(lax.ppermute(earlier[-1], 'feat', up))]
    ppermute x0 -> x7, starting transfers between devices: none -> 16.3 us  [the longest x3 8.9 us: local(): later.append(lax.ppermute(later[-1], 'feat', down))]
    ppermute x0 -> x7, waiting for transfers between devices: none -> 9.39 us  [the longest x4 9.38 us: local(): earlier.append(lax.ppermute(earlier[-1], 'feat', up))]
    psum x1, waiting for transfers between devices: 83.7 us -> 92.1 us  [local(): lax.psum((wself_full, wneigh_full, bias_grad), ('grp', 'feat'))]
    psum x1, blocking collectives: 39.1 us -> 43 us  [local(): lax.psum((wself_full, wneigh_full, bias_grad), ('grp', 'feat'))]
  transfers between devices with their start and end apart: 4 -> 10, of which waited for: 4 -> 5; matrix products, arithmetic and copies ran while one was open for 3% -> 9% of each run, Pallas kernels for 0% -> 0%
where the time goes in v1:
time: 273 us; the launch traced here: 271 us
  waiting for transfers between devices  119 us (44%)
  local copies, waits for them, and re-layouts  58.3 us (21%)
  blocking collectives  49.3 us (18%)
  starting transfers between devices  16.4 us (6%)
  between operations  15.8 us (6%)
  matrix products  8.21 us (3%)
  other arithmetic  4.02 us (1%)
    psum x1, waiting for transfers between devices, local(): lax.psum((wself_full, wneigh_full, bias_grad), ('grp', 'feat'))  92.1 us
    psum x1, blocking collectives, local(): lax.psum((wself_full, wneigh_full, bias_grad), ('grp', 'feat'))  43 us
    concatenate x1, local copies, waits for them, and re-layouts, local(): jnp.roll(line, (lax.axis_index('feat') - ways // 2) * combined.shape[0],...  20.2 us
    reduce_scatter x1, waiting for transfers between devices, local(): lax.psum_scatter(hub_part.astype(jnp.bfloat16), 'grp', scatter_dimension=...  17.5 us
    ppermute x4, local copies, waits for them, and re-layouts, local(): earlier.append(lax.ppermute(earlier[-1], 'feat', up))  9.61 us
    ppermute x4, waiting for transfers between devices, local(): earlier.append(lax.ppermute(earlier[-1], 'feat', up))  9.38 us
    ppermute x3, starting transfers between devices, local(): later.append(lax.ppermute(later[-1], 'feat', down))  8.9 us
    ppermute x4, starting transfers between devices, local(): earlier.append(lax.ppermute(earlier[-1], 'feat', up))  7.39 us
  transfers between devices with their start and end apart: 10, of which 5 were waited for; matrix products, arithmetic and copies ran while one was open for 9% of the time, Pallas kernels for 0%

profile of v1, /device:TPU:0, one launch (start us, length us, event | category | flops | bytes accessed | tf_op | source)
XLA Modules:
  0.0 271.0 jit_solution(16599675943716961695)
XLA Ops:
  8.0 0.0 all-reduce.3.cloned.1.call-start
  8.1 1.1 constant_dynamic-update-slice_fusion.1
  9.1 0.9 copy_bitcast_fusion.3
  10.0 0.7 compare_and_fusion.2
  10.7 0.7 fusion.36
  11.4 0.1 broadcast_bitcast_fusion
  11.5 0.6 gather_fusion
  12.0 6.2 %all_gather.3 = bf16[16,1024]{1,0:T(8,128)(2,1)S(1)} all-gather(bf16[16,256]{1,0:T(8,128)(2,1)S(1)} %bitcast_select_fusion), channel_id=1, replica_groups=mesh['grp'=4,'feat'=8] {'grp'}, dimensions={1}, use_global_device_ids=true | all-gather | bytes 40960 | tf_op jit(solution)/shard_map/all_gather | solution.py:49
  18.3 1.9 collective-permute-start
  20.2 3.1 %collective-permute-start.4 = (bf16[16,5120]{1,0:T(8,128)(2,1)S(1)}, bf16[16,5120]{1,0:T(8,128)(2,1)S(1)}, u32[]{:S(2)}, u32[]{:S(2)}) collective-permute-start(bf16[16,5120]{1,0:T(8,128)(2,1)S(1)} %constant_dynamic-update-slice_fusion), channel_id=1, source_target_pairs={{0,7},{1,0},{2,1},{3,2},{4,3},{5,4},{6,5},{7,6},{8,15},{9,8},{10,9... | collective-permute-start | bytes 491528 | tf_op jit(solution)/shard_map/ppermute | solution.py:60
  23.3 4.8 %collective-permute-done = bf16[16,5120]{1,0:T(8,128)(2,1)S(1)} collective-permute-done((bf16[16,5120]{1,0:T(8,128)(2,1)S(1)}, bf16[16,5120]{1,0:T(8,128)(2,1)S(1)}, u32[]{:S(2)}, u32[]{:S(2)}) %collective-permute-start) | collective-permute-done | bytes 163872 | tf_op jit(solution)/shard_map/ppermute | solution.py:58
  28.0 2.1 collective-permute-start.1
  30.1 0.7 compare_and_fusion
  30.9 3.1 %collective-permute-start.5 = (bf16[16,5120]{1,0:T(8,128)(2,1)S(1)}, bf16[16,5120]{1,0:T(8,128)(2,1)}, u32[]{:S(2)}, u32[]{:S(2)}) collective-permute-start(bf16[16,5120]{1,0:T(8,128)(2,1)S(1)} %collective-permute-done.4), channel_id=1, source_target_pairs={{0,7},{1,0},{2,1},{3,2},{4,3},{5,4},{6,5},{7,6},{8,15},{9,8},{10,9... | collective-permute-start | bytes 491528 | tf_op jit(solution)/shard_map/ppermute | solution.py:60
  34.0 3.2 %collective-permute-done.1 = bf16[16,5120]{1,0:T(8,128)(2,1)S(1)} collective-permute-done((bf16[16,5120]{1,0:T(8,128)(2,1)S(1)}, bf16[16,5120]{1,0:T(8,128)(2,1)S(1)}, u32[]{:S(2)}, u32[]{:S(2)}) %collective-permute-start.1) | collective-permute-done | bytes 163872 | tf_op jit(solution)/shard_map/ppermute | solution.py:58
  37.2 2.1 collective-permute-start.2
  39.3 0.7 fusion.37
  40.0 1.2 constant_dynamic-slice_fusion.3
  41.3 2.7 collective-permute-start.6
  43.9 1.4 collective-permute-done.2
  45.4 1.3 collective-permute-start.3
  46.6 0.7 compare_convert_fusion
  47.3 1.5 copy.41
  48.8 2.4 copy.40
  51.2 2.4 copy.42
  53.6 2.4 copy.39
  56.0 2.5 copy.43
  58.5 2.4 copy.38
  60.9 2.4 copy.44
  63.3 2.4 copy.37
  65.7 20.2 %concatenate.10 = bf16[256,5120]{0,1:T(8,128)(2,1)} concatenate(bf16[16,5120]{0,1:T(8,128)(2,1)} %copy.37, bf16[16,5120]{0,1:T(8,128)(2,1)} %copy.38, bf16[16,5120]{0,1:T(8,128)(2,1)} %copy.39, bf16[16,5120]{0,1:T(8,128)(2,1)} %copy.40, bf16[16,5120]{0,1:T(8,128)(2,1)S(1)} %copy.41, bf16[16,5120]{0,1:T(8,128)(2,1)} %copy.42, bf16[16,5120]{0,1:T(8,128)(2,1)} %copy.43, ...), dimensions={0} | concatenate | bytes 5242880 | tf_op jit(solution)/shard_map/jit(_roll_dynamic)/concatenate | solution.py:62
  85.9 2.2 constant_dynamic-slice_fusion.4
  88.1 1.5 copy.53
  89.6 2.0 gather_fusion.1
  91.6 0.4 fusion.1
  91.9 0.7 convolution_convert_fusion.1
  92.6 0.3 fusion.19
  92.9 2.1 convert_reduce_fusion
  95.0 0.2 convolution_convert_fusion
  95.2 1.9 fusion.25
  97.2 0.8 fusion.17
  98.0 0.1 copy.55
  98.2 0.6 gather_fusion.2
  98.8 0.3 fusion
  99.0 1.3 fusion.4
  100.4 0.5 copy.86
  100.8 1.5 copy-done.1
  102.4 0.1 copy.62
  102.5 0.0 all-reduce.3.cloned.1.call-update
  102.5 0.0 reduce-scatter.3.cloned.1.call-start
  102.6 0.2 fusion.3
  102.8 0.1 copy.58
  102.9 0.8 constant_dynamic-update-slice_fusion.2
  103.7 0.0 reduce-scatter.5.cloned.1.call-start
  103.8 43.0 %psum.23 = f32[256]{0:T(256)} all-reduce(f32[256]{0:T(256)S(1)} %get-tuple-element.7), channel_id=1, replica_groups=mesh['grp'=4,'feat'=8] {'grp','feat'}, use_global_device_ids=true, to_apply=%region_6.7 | all-reduce | flops 256 | bytes 2048 | tf_op jit(solution)/shard_map/psum | solution.py:90
  146.8 92.1 %all-reduce.3.cloned.1.call-done = (f32[128,256]{1,0:T(8,128)}, f32[128,256]{1,0:T(8,128)}) async-done(((f32[128,256]{1,0:T(8,128)}, f32[128,256]{1,0:T(8,128)}), (f32[128,256]{1,0:T(8,128)}, f32[128,256]{1,0:T(8,128)})) %all-reduce.3.cloned.1.call-update) | async-done | bytes 262160 | tf_op jit(solution)/shard_map/psum | solution.py:90
  238.9 1.3 constant_dynamic-slice_fusion.1
  240.2 1.3 constant_dynamic-slice_fusion
  241.6 1.5 slice.19
  243.1 1.0 copy_bitcast_fusion.2
  244.0 17.5 %reduce-scatter.5.cloned.1.call-done = bf16[16,256]{1,0:T(8,128)(2,1)} async-done(((bf16[16,1024]{1,0:T(8,128)(2,1)}), bf16[16,256]{1,0:T(8,128)(2,1)}) %reduce-scatter.5.cloned.1.call-update) | async-done | bytes 8208 | tf_op jit(solution)/shard_map/reduce_scatter | solution.py:114
  261.5 0.7 reshape.194
  262.2 0.6 scatter_fusion
  262.9 0.7 copy_bitcast_fusion.1
  (33 shorter events, 0.1 us)
Async XLA Ops:
  8.0 83.5 %copy-start = (bf16[1,8,8,128,128]{4,3,2,1,0:T(8,128)(2,1)S(1)}, bf16[1,8,8,128,128]{4,3,2,1,0:T(8,128)(2,1)}, u32[]{:S(2)}) copy-start(bf16[1,8,8,128,128]{4,3,2,1,0:T(8,128)(2,1)} %param.14) | copy-start | bytes 6291460
  8.0 230.9 %all-reduce.3.cloned.1.call-start = ((), (), s32[]{:S(2)}) async-start(), calls=%async_computation.4 | async-start | bytes 524288 | tf_op jit(solution)/shard_map/psum | solution.py:90
  18.3 28.4 %copy-start.2 = (bf16[16,5120]{1,0:T(8,128)(2,1)}, bf16[16,5120]{1,0:T(8,128)(2,1)S(1)}, u32[]{:S(2)}) copy-start(bf16[16,5120]{1,0:T(8,128)(2,1)S(1)} %constant_dynamic-update-slice_fusion) | copy-start | bytes 491524
  18.3 9.8 %collective-permute-start = (bf16[16,5120]{1,0:T(8,128)(2,1)S(1)}, bf16[16,5120]{1,0:T(8,128)(2,1)S(1)}, u32[]{:S(2)}, u32[]{:S(2)}) collective-permute-start(bf16[16,5120]{1,0:T(8,128)(2,1)S(1)} %constant_dynamic-update-slice_fusion), channel_id=1, source_target_pairs={{0,1},{1,2},{2,3},{3,4},{4,5},{5,6},{6,7},{7,0},{8,9},{9,10},{10,1... | collective-permute-start | bytes 491528 | tf_op jit(solution)/shard_map/ppermute | solution.py:58
  20.2 10.7 %collective-permute-start.4 = (bf16[16,5120]{1,0:T(8,128)(2,1)S(1)}, bf16[16,5120]{1,0:T(8,128)(2,1)S(1)}, u32[]{:S(2)}, u32[]{:S(2)}) collective-permute-start(bf16[16,5120]{1,0:T(8,128)(2,1)S(1)} %constant_dynamic-update-slice_fusion), channel_id=1, source_target_pairs={{0,7},{1,0},{2,1},{3,2},{4,3},{5,4},{6,5},{7,6},{8,15},{9,8},{10,9... | collective-permute-start | bytes 491528 | tf_op jit(solution)/shard_map/ppermute | solution.py:60
  28.0 18.6 %copy-start.4 = (bf16[16,5120]{1,0:T(8,128)(2,1)}, bf16[16,5120]{1,0:T(8,128)(2,1)S(1)}, u32[]{:S(2)}) copy-start(bf16[16,5120]{1,0:T(8,128)(2,1)S(1)} %collective-permute-done) | copy-start | bytes 491524
  28.0 9.2 %collective-permute-start.1 = (bf16[16,5120]{1,0:T(8,128)(2,1)S(1)}, bf16[16,5120]{1,0:T(8,128)(2,1)S(1)}, u32[]{:S(2)}, u32[]{:S(2)}) collective-permute-start(bf16[16,5120]{1,0:T(8,128)(2,1)S(1)} %collective-permute-done), channel_id=1, source_target_pairs={{0,1},{1,2},{2,3},{3,4},{4,5},{5,6},{6,7},{7,0},{8,9},{9,10},{10,1... | collective-permute-start | bytes 491528 | tf_op jit(solution)/shard_map/ppermute | solution.py:58
  30.9 15.8 %copy-start.5 = (bf16[16,5120]{1,0:T(8,128)(2,1)}, bf16[16,5120]{1,0:T(8,128)(2,1)S(1)}, u32[]{:S(2)}) copy-start(bf16[16,5120]{1,0:T(8,128)(2,1)S(1)} %collective-permute-done.4) | copy-start | bytes 491524
  30.9 10.4 %collective-permute-start.5 = (bf16[16,5120]{1,0:T(8,128)(2,1)S(1)}, bf16[16,5120]{1,0:T(8,128)(2,1)}, u32[]{:S(2)}, u32[]{:S(2)}) collective-permute-start(bf16[16,5120]{1,0:T(8,128)(2,1)S(1)} %collective-permute-done.4), channel_id=1, source_target_pairs={{0,7},{1,0},{2,1},{3,2},{4,3},{5,4},{6,5},{7,6},{8,15},{9,8},{10,9... | collective-permute-start | bytes 491528 | tf_op jit(solution)/shard_map/ppermute | solution.py:60
  37.2 9.4 %copy-start.6 = (bf16[16,5120]{1,0:T(8,128)(2,1)}, bf16[16,5120]{1,0:T(8,128)(2,1)S(1)}, u32[]{:S(2)}) copy-start(bf16[16,5120]{1,0:T(8,128)(2,1)S(1)} %collective-permute-done.1) | copy-start | bytes 491524
  37.2 8.2 %collective-permute-start.2 = (bf16[16,5120]{1,0:T(8,128)(2,1)S(1)}, bf16[16,5120]{1,0:T(8,128)(2,1)}, u32[]{:S(2)}, u32[]{:S(2)}) collective-permute-start(bf16[16,5120]{1,0:T(8,128)(2,1)S(1)} %collective-permute-done.1), channel_id=1, source_target_pairs={{0,1},{1,2},{2,3},{3,4},{4,5},{5,6},{6,7},{7,0},{8,9},{9,10},{10,1... | collective-permute-start | bytes 491528 | tf_op jit(solution)/shard_map/ppermute | solution.py:58
  41.3 19.7 %collective-permute-start.6 = (bf16[16,5120]{1,0:T(8,128)(2,1)}, bf16[16,5120]{1,0:T(8,128)(2,1)}, u32[]{:S(2)}, u32[]{:S(2)}) collective-permute-start(bf16[16,5120]{1,0:T(8,128)(2,1)} %collective-permute-done.5), channel_id=1, source_target_pairs={{0,7},{1,0},{2,1},{3,2},{4,3},{5,4},{6,5},{7,6},{8,15},{9,8},{10,9... | collective-permute-start | bytes 491528 | tf_op jit(solution)/shard_map/ppermute | solution.py:60
  45.4 17.9 %collective-permute-start.3 = (bf16[16,5120]{1,0:T(8,128)(2,1)}, bf16[16,5120]{1,0:T(8,128)(2,1)}, u32[]{:S(2)}, u32[]{:S(2)}) collective-permute-start(bf16[16,5120]{1,0:T(8,128)(2,1)} %collective-permute-done.2), channel_id=1, source_target_pairs={{0,1},{1,2},{2,3},{3,4},{4,5},{5,6},{6,7},{7,0},{8,9},{9,10},{10,1... | collective-permute-start | bytes 491528 | tf_op jit(solution)/shard_map/ppermute | solution.py:58
  88.1 4.5 %copy-start.3 = (bf16[128,256]{1,0:T(8,128)(2,1)S(1)}, bf16[128,256]{1,0:T(8,128)(2,1)}, u32[]{:S(2)}) copy-start(bf16[128,256]{1,0:T(8,128)(2,1)} %param.12) | copy-start | bytes 196612
  89.6 3.3 %copy-start.7 = (bf16[128,256]{1,0:T(8,128)(2,1)S(1)}, bf16[128,256]{1,0:T(8,128)(2,1)}, u32[]{:S(2)}) copy-start(bf16[128,256]{1,0:T(8,128)(2,1)} %param.11) | copy-start | bytes 196612
  89.6 3.3 %copy-start.8 = (bf16[512,256]{1,0:T(8,128)(2,1)S(1)}, bf16[512,256]{1,0:T(8,128)(2,1)}, u32[]{:S(2)}) copy-start(bf16[512,256]{1,0:T(8,128)(2,1)} %param.19) | copy-start | bytes 786436
  89.6 3.3 %copy-start.9 = (f32[256]{0:T(256)S(1)}, f32[256]{0:T(256)}, u32[]{:S(2)}) copy-start(f32[256]{0:T(256)} %param.13) | copy-start | bytes 3076
  100.8 1.5 copy-start.1
  102.5 139.1 %reduce-scatter.3.cloned.1.call-start = ((), (), s32[]{:S(2)}) async-start(), calls=%async_computation.2 | async-start | bytes 2949120 | tf_op jit(solution)/shard_map/reduce_scatter | solution.py:110
  103.7 157.8 %reduce-scatter.5.cloned.1.call-start = ((), (), s32[]{:S(2)}) async-start(), calls=%async_computation.3 | async-start | bytes 40960 | tf_op jit(solution)/shard_map/reduce_scatter | solution.py:114
Sparse Core Ops, SparseCore 0:
  102.6 136.2 all-reduce.2
Sparse Core Ops, SparseCore 1:
  106.5 72.4 reduce-scatter.2
  243.1 18.3 reduce-scatter.4
